TPU v7x, 32 devices: a whole 2x2x4 slice. The times are simulated.
32 devices in a mesh: panel: 8 (over y, x, core), hist: 4 (over z).
Axes of the slice: x: 2, y: 2, z: 4, core: 2. Of those that a mesh axis runs over, the one named last changes fastest.
Arguments:
- excitation: bfloat16 [2, 32, 128, 128], P(None, 'panel'), may hold values from -8 to 8
- past: bfloat16 [16, 32, 128, 128], P('hist', 'panel'), may hold values from -6 to 6
- hist_tiles: bfloat16 [16, 32, 5, 128, 128], P('hist', 'panel'), may hold values from -0.078125 to 0.078125
- hist_src: int32 [16, 32, 5], P('hist', 'panel'), may hold values from -4 to 4, as said below
- hist_count: int32 [16, 32], P('hist', 'panel'), may hold values from 1 to 5, as said below
- near_tiles: bfloat16 [32, 3, 128, 128], P('panel'), may hold values from -0.5 to 4, as said below
Outputs:
- currents: bfloat16 [2, 32, 128, 128], P(None, 'panel', None, 'hist')
Inputs may be any that keep to these rules, and one draw needn't show every extreme that they name: `hist_src`: the offsets within one shell and target block are distinct. `hist_count`: in every shell some block has all 5 slots live. The diagonal entries of every near_tiles[n, 1] lie between 2 and 4.
All inputs are finite; a program needn't handle non-finite values.
Results may differ from a plain program's by a relative error of at most 0.0054.
Values may be sent and summed in bfloat16 or wider, within the bound.
A program may use at most 64 MiB of HBM per device.

v0:
```python
import jax
import jax.numpy as jnp
from jax import lax
from jax.sharding import PartitionSpec as P

WIN = 4
TPB = 5
SWEEPS = 3


def extended(block, sides, width):
    for axis, dim in sides:
        count = lax.axis_size(axis)
        forward = [(i, i + 1) for i in range(count - 1)]
        backward = [(target, source) for source, target in forward]
        low = lax.ppermute(
            lax.slice_in_dim(block, block.shape[dim] - width, None, axis=dim), axis, forward
        )
        high = lax.ppermute(lax.slice_in_dim(block, 0, width, axis=dim), axis, backward)
        block = jnp.concatenate([low, block, high], axis=dim)
    return block


def shifted_2(value, axis, by):
    peers = lax.axis_size(axis)
    pairs = [(i, i + by) for i in range(peers) if 0 <= i + by < peers]
    return lax.ppermute(value, axis, pairs)


def shell_field(shell_rim, tiles, source, count):
    blocks = tiles.shape[0]
    index = jnp.arange(blocks, dtype=jnp.int32)[:, None] + WIN + source
    taken = shell_rim[index]
    live = jnp.arange(TPB, dtype=jnp.int32)[None, :] < count[:, None]
    taken = jnp.where(live[:, :, None, None], taken, jnp.zeros((), jnp.bfloat16))
    return jnp.einsum("nsij,nsjp->nip", tiles, taken, preferred_element_type=jnp.float32)


def jacobi(drive, near_tiles, diag):
    state = drive / diag
    blocks = drive.shape[0]
    for sweep in range(SWEEPS - 1):
        rounded = state.astype(jnp.bfloat16)
        padded = extended(rounded, (("panel", 0),), 1)
        applied = jnp.einsum(
            "nij,njp->nip", near_tiles[:, 0], padded[0:blocks], preferred_element_type=jnp.float32
        )
        applied = applied + jnp.einsum(
            "nij,njp->nip",
            near_tiles[:, 1],
            padded[1 : blocks + 1],
            preferred_element_type=jnp.float32,
        )
        applied = applied + jnp.einsum(
            "nij,njp->nip",
            near_tiles[:, 2],
            padded[2 : blocks + 2],
            preferred_element_type=jnp.float32,
        )
        state = state + (drive - applied) / diag
    return state.astype(jnp.bfloat16)


def settle(partial_value, incident, near_tiles, diag):
    field = lax.psum(partial_value, "hist")
    return jacobi(incident.astype(jnp.float32) - field, near_tiles, diag)


def shards(excitation, past, hist_tiles, hist_src, hist_count, near_tiles):
    shells = past.shape[0]
    ports = past.shape[3]
    share = ports // lax.axis_size("hist")
    hist_pos = lax.axis_index("hist")
    diag = jnp.diagonal(near_tiles[:, 1], axis1=1, axis2=2).astype(jnp.float32)[:, :, None]
    rim = extended(past, (("panel", 1),), WIN)
    partial_one = shell_field(rim[0], hist_tiles[0], hist_src[0], hist_count[0])
    for shell in range(1, shells):
        partial_one = partial_one + shell_field(
            rim[shell], hist_tiles[shell], hist_src[shell], hist_count[shell]
        )
    partial_two = shell_field(rim[0], hist_tiles[1], hist_src[1], hist_count[1])
    for shell in range(2, shells):
        partial_two = partial_two + shell_field(
            rim[shell - 1], hist_tiles[shell], hist_src[shell], hist_count[shell]
        )
    first = settle(partial_one, excitation[0], near_tiles, diag)
    shifted = shifted_2(rim[shells - 1], "hist", 1)
    new_rim = extended(first, (("panel", 0),), WIN)
    incoming = jnp.where(hist_pos == 0, new_rim, shifted)
    partial_two = partial_two + shell_field(incoming, hist_tiles[0], hist_src[0], hist_count[0])
    second = settle(partial_two, excitation[1], near_tiles, diag)
    first_mine = lax.dynamic_slice_in_dim(first, hist_pos * share, share, 2)
    second_mine = lax.dynamic_slice_in_dim(second, hist_pos * share, share, 2)
    return jnp.stack([first_mine, second_mine], axis=0)


def solution(mesh):
    return jax.shard_map(
        shards,
        mesh=mesh,
        in_specs=(
            P(None, "panel", None, None),
            P("hist", "panel", None, None),
            P("hist", "panel", None, None, None),
            P("hist", "panel", None),
            P("hist", "panel"),
            P("panel", None, None, None),
        ),
        out_specs=P(None, "panel", None, "hist"),
        check_vma=False,
    )
```

profile of v0, /device:TPU:4, one launch (start us, length us, event | category | flops | bytes accessed | tf_op | source)
XLA Modules:
  0.0 167.2 jit_solution(1262591120672399657)
XLA Ops:
  7.9 2.9 %collective-permute-start.1 = (bf16[4,4,128,128]{2,3,1,0:T(8,128)(2,1)S(1)}, bf16[4,4,128,128]{2,3,1,0:T(8,128)(2,1)S(1)}, u32[]{:S(2)}, u32[]{:S(2)}) collective-permute-start(bf16[4,4,128,128]{2,3,1,0:T(8,128)(2,1)S(1)} %copy.8), channel_id=1, source_target_pairs={{4,0},{8,4},{12,8},{16,12},{20,16},{24,20},{28,24},{5,1},{9,5},{13... | collective-permute-start | bytes 1572872 | tf_op jit(solution)/shard_map/ppermute | solution.py:19
  10.8 1.9 %collective-permute-start = (bf16[4,4,128,128]{2,3,1,0:T(8,128)(2,1)S(1)}, bf16[4,4,128,128]{2,3,1,0:T(8,128)(2,1)S(1)}, u32[]{:S(2)}, u32[]{:S(2)}) collective-permute-start(bf16[4,4,128,128]{2,3,1,0:T(8,128)(2,1)S(1)} %copy.8), channel_id=1, source_target_pairs={{0,4},{4,8},{8,12},{12,16},{16,20},{20,24},{24,28},{1,5},{5,9},{9,... | collective-permute-start | bytes 1572872 | tf_op jit(solution)/shard_map/ppermute | solution.py:16
  13.7 3.2 %copy.12 = bf16[4,128,128]{0,2,1:T(8,128)(2,1)} copy(bf16[4,128,128]{2,1,0:T(8,128)(2,1)S(1)} %slice_bitcast_fusion.4) | data formatting | bytes 262144 | tf_op jit(solution)/shard_map/squeeze | solution.py:74
  16.9 1.9 %gather_fusion.4 = bf16[128,4]{1,0:T(8,128)(2,1)S(1)} fusion(bf16[4,128,128]{0,2,1:T(8,128)(2,1)} %copy.12, s32[128]{0:T(128)S(1)} %or_bitcast_fusion), kind=kCustom, calls=%fused_computation.4 | custom fusion | bytes 3072 | tf_op jit(solution)/shard_map/jit(diagonal)/gather | solution.py:74
  21.1 3.1 %collective-permute-done = bf16[4,4,128,128]{2,3,1,0:T(8,128)(2,1)S(1)} collective-permute-done((bf16[4,4,128,128]{2,3,1,0:T(8,128)(2,1)S(1)}, bf16[4,4,128,128]{2,3,1,0:T(8,128)(2,1)S(1)}, u32[]{:S(2)}, u32[]{:S(2)}) %collective-permute-start) | collective-permute-done | bytes 524320 | tf_op jit(solution)/shard_map/ppermute | solution.py:16
  24.4 4.2 %collective-permute-start.8 = (bf16[12,128,128]{1,2,0:T(8,128)(2,1)S(1)}, bf16[12,128,128]{1,2,0:T(8,128)(2,1)}, u32[]{:S(2)}, u32[]{:S(2)}) collective-permute-start(bf16[12,128,128]{1,2,0:T(8,128)(2,1)S(1)} %get-tuple-element.7), channel_id=1, source_target_pairs={{0,1},{1,2},{2,3},{4,5},{5,6},{6,7},{8,9},{9,10},{10,11},{12,13},{... | collective-permute-start | bytes 1179656 | tf_op jit(solution)/shard_map/ppermute | solution.py:27
  30.0 1.5 gather_fusion.2
  32.2 1.5 gather_fusion.1
  33.8 1.5 gather_fusion
  35.3 1.6 convolution_bitcast_fusion.4
  36.9 1.8 %convolution_bitcast_fusion.5 = f32[4,128,128]{2,1,0:T(8,128)S(1)} fusion(bf16[4,5,128,128]{2,3,1,0:T(8,128)(2,1)} %bitcast.202, pred[4,5]{1,0:T(4,128)(4,1)S(1)} %get-tuple-element.34, bf16[4,4,5,128,128]{4,3,2,1,0:T(8,128)(2,1)} %param.8), kind=kOutput, calls=%fused_computation.30 | convolution fusion | flops 84213760 | bytes 1572884 | tf_op jit(solution)/shard_map/nsij,nsjp->nip/dot_general | solution.py:36
  40.3 1.5 convolution_bitcast_fusion.1
  42.5 1.5 convolution_bitcast_fusion.2
  44.0 31.1 %all-reduce.3.cloned.1.call-done = f32[4,128,128]{1,2,0:T(8,128)} async-done(((f32[4,128,128]{1,2,0:T(8,128)}), f32[4,128,128]{1,2,0:T(8,128)}) %all-reduce.3.cloned.1.call-update) | async-done | bytes 262160 | tf_op jit(solution)/shard_map/psum | solution.py:65
  76.2 2.1 %collective-permute-start.3 = (bf16[1,128,128]{1,2,0:T(8,128)(2,1)S(1)}, bf16[1,128,128]{1,2,0:T(8,128)(2,1)S(1)}, u32[]{:S(2)}, u32[]{:S(2)}) collective-permute-start(bf16[1,128,128]{1,2,0:T(8,128)(2,1)S(1)} %get-tuple-element.20), channel_id=1, source_target_pairs={{4,0},{8,4},{12,8},{16,12},{20,16},{24,20},{28,24},{5,1},{9,5},{13... | collective-permute-start | bytes 98312 | tf_op jit(solution)/shard_map/ppermute | solution.py:19
  78.4 2.4 %collective-permute-start.2 = (bf16[1,128,128]{1,2,0:T(8,128)(2,1)S(1)}, bf16[1,128,128]{1,2,0:T(8,128)(2,1)S(1)}, u32[]{:S(2)}, u32[]{:S(2)}) collective-permute-start(bf16[1,128,128]{1,2,0:T(8,128)(2,1)S(1)} %get-tuple-element.19), channel_id=1, source_target_pairs={{0,4},{4,8},{8,12},{12,16},{16,20},{20,24},{24,28},{1,5},{5,9},{9,... | collective-permute-start | bytes 98312 | tf_op jit(solution)/shard_map/ppermute | solution.py:16
  81.1 3.5 %collective-permute-done.2 = bf16[1,128,128]{1,2,0:T(8,128)(2,1)S(1)} collective-permute-done((bf16[1,128,128]{1,2,0:T(8,128)(2,1)S(1)}, bf16[1,128,128]{1,2,0:T(8,128)(2,1)S(1)}, u32[]{:S(2)}, u32[]{:S(2)}) %collective-permute-start.2) | collective-permute-done | bytes 32800 | tf_op jit(solution)/shard_map/ppermute | solution.py:16
  85.8 1.9 %collective-permute-start.5 = (bf16[1,128,128]{1,2,0:T(8,128)(2,1)S(1)}, bf16[1,128,128]{1,2,0:T(8,128)(2,1)S(1)}, u32[]{:S(2)}, u32[]{:S(2)}) collective-permute-start(bf16[1,128,128]{1,2,0:T(8,128)(2,1)S(1)} %get-tuple-element.18), channel_id=1, source_target_pairs={{4,0},{8,4},{12,8},{16,12},{20,16},{24,20},{28,24},{5,1},{9,5},{13... | collective-permute-start | bytes 98312 | tf_op jit(solution)/shard_map/ppermute | solution.py:19
  87.9 2.4 %collective-permute-start.4 = (bf16[1,128,128]{1,2,0:T(8,128)(2,1)S(1)}, bf16[1,128,128]{1,2,0:T(8,128)(2,1)S(1)}, u32[]{:S(2)}, u32[]{:S(2)}) collective-permute-start(bf16[1,128,128]{1,2,0:T(8,128)(2,1)S(1)} %get-tuple-element.17), channel_id=1, source_target_pairs={{0,4},{4,8},{8,12},{12,16},{16,20},{20,24},{24,28},{1,5},{5,9},{9,... | collective-permute-start | bytes 98312 | tf_op jit(solution)/shard_map/ppermute | solution.py:16
  90.6 3.5 %collective-permute-done.4 = bf16[1,128,128]{1,2,0:T(8,128)(2,1)S(1)} collective-permute-done((bf16[1,128,128]{1,2,0:T(8,128)(2,1)S(1)}, bf16[1,128,128]{1,2,0:T(8,128)(2,1)S(1)}, u32[]{:S(2)}, u32[]{:S(2)}) %collective-permute-start.4) | collective-permute-done | bytes 32800 | tf_op jit(solution)/shard_map/ppermute | solution.py:16
  94.3 1.9 %collective-permute-start.7 = (bf16[4,128,128]{1,2,0:T(8,128)(2,1)S(1)}, bf16[4,128,128]{1,2,0:T(8,128)(2,1)S(1)}, u32[]{:S(2)}, u32[]{:S(2)}) collective-permute-start(bf16[4,128,128]{1,2,0:T(8,128)(2,1)S(1)} %fusion.25), channel_id=1, source_target_pairs={{4,0},{8,4},{12,8},{16,12},{20,16},{24,20},{28,24},{5,1},{9,5},{13... | collective-permute-start | bytes 393224 | tf_op jit(solution)/shard_map/ppermute | solution.py:19
  96.2 2.4 %collective-permute-start.6 = (bf16[4,128,128]{1,2,0:T(8,128)(2,1)S(1)}, bf16[4,128,128]{1,2,0:T(8,128)(2,1)S(1)}, u32[]{:S(2)}, u32[]{:S(2)}) collective-permute-start(bf16[4,128,128]{1,2,0:T(8,128)(2,1)S(1)} %fusion.25), channel_id=1, source_target_pairs={{0,4},{4,8},{8,12},{12,16},{16,20},{20,24},{24,28},{1,5},{5,9},{9,... | collective-permute-start | bytes 393224 | tf_op jit(solution)/shard_map/ppermute | solution.py:16
  98.6 1.5 fusion.22
  100.2 3.2 %collective-permute-done.6 = bf16[4,128,128]{1,2,0:T(8,128)(2,1)S(1)} collective-permute-done((bf16[4,128,128]{1,2,0:T(8,128)(2,1)S(1)}, bf16[4,128,128]{1,2,0:T(8,128)(2,1)S(1)}, u32[]{:S(2)}, u32[]{:S(2)}) %collective-permute-start.6) | collective-permute-done | bytes 131104 | tf_op jit(solution)/shard_map/ppermute | solution.py:16
  104.1 2.2 %fusion.24 = f32[4,128,128]{1,2,0:T(8,128)} fusion(f32[4,128,128]{2,1,0:T(8,128)S(1)} %fusion.22, bf16[4,5,128,128]{2,3,1,0:T(8,128)(2,1)S(1)} %bitcast.205, pred[4,5]{1,0:T(4,128)(4,1)S(1)} %iota_compare_fusion.3, bf16[4,4,5,128,128]{4,3,2,1,0:T(8,128)(2,1)} %param.8), kind=kOutput, calls=%fused_computation.46 | convolution fusion | flops 84279296 | bytes 1835028 | tf_op jit(solution)/shard_map/nsij,nsjp->nip/dot_general | solution.py:36
  106.5 35.1 %all-reduce.5.cloned.1.call-done = f32[4,128,128]{1,2,0:T(8,128)} async-done(((f32[4,128,128]{1,2,0:T(8,128)}), f32[4,128,128]{1,2,0:T(8,128)}) %all-reduce.5.cloned.1.call-update) | async-done | bytes 262160 | tf_op jit(solution)/shard_map/psum | solution.py:65
  142.7 1.9 %collective-permute-start.10 = (bf16[1,128,128]{1,2,0:T(8,128)(2,1)S(1)}, bf16[1,128,128]{1,2,0:T(8,128)(2,1)S(1)}, u32[]{:S(2)}, u32[]{:S(2)}) collective-permute-start(bf16[1,128,128]{1,2,0:T(8,128)(2,1)S(1)} %get-tuple-element.16), channel_id=1, source_target_pairs={{4,0},{8,4},{12,8},{16,12},{20,16},{24,20},{28,24},{5,1},{9,5},{13... | collective-permute-start | bytes 98312 | tf_op jit(solution)/shard_map/ppermute | solution.py:19
  144.8 2.4 %collective-permute-start.9 = (bf16[1,128,128]{1,2,0:T(8,128)(2,1)S(1)}, bf16[1,128,128]{1,2,0:T(8,128)(2,1)S(1)}, u32[]{:S(2)}, u32[]{:S(2)}) collective-permute-start(bf16[1,128,128]{1,2,0:T(8,128)(2,1)S(1)} %get-tuple-element.15), channel_id=1, source_target_pairs={{0,4},{4,8},{8,12},{12,16},{16,20},{20,24},{24,28},{1,5},{5,9},{9,... | collective-permute-start | bytes 98312 | tf_op jit(solution)/shard_map/ppermute | solution.py:16
  147.5 3.5 %collective-permute-done.9 = bf16[1,128,128]{1,2,0:T(8,128)(2,1)S(1)} collective-permute-done((bf16[1,128,128]{1,2,0:T(8,128)(2,1)S(1)}, bf16[1,128,128]{1,2,0:T(8,128)(2,1)S(1)}, u32[]{:S(2)}, u32[]{:S(2)}) %collective-permute-start.9) | collective-permute-done | bytes 32800 | tf_op jit(solution)/shard_map/ppermute | solution.py:16
  151.2 1.9 %collective-permute-start.12 = (bf16[1,128,128]{1,2,0:T(8,128)(2,1)S(1)}, bf16[1,128,128]{1,2,0:T(8,128)(2,1)S(1)}, u32[]{:S(2)}, u32[]{:S(2)}) collective-permute-start(bf16[1,128,128]{1,2,0:T(8,128)(2,1)S(1)} %get-tuple-element.14), channel_id=1, source_target_pairs={{4,0},{8,4},{12,8},{16,12},{20,16},{24,20},{28,24},{5,1},{9,5},{13... | collective-permute-start | bytes 98312 | tf_op jit(solution)/shard_map/ppermute | solution.py:19
  153.4 2.4 %collective-permute-start.11 = (bf16[1,128,128]{1,2,0:T(8,128)(2,1)S(1)}, bf16[1,128,128]{1,2,0:T(8,128)(2,1)S(1)}, u32[]{:S(2)}, u32[]{:S(2)}) collective-permute-start(bf16[1,128,128]{1,2,0:T(8,128)(2,1)S(1)} %get-tuple-element.13), channel_id=1, source_target_pairs={{0,4},{4,8},{8,12},{12,16},{16,20},{20,24},{24,28},{1,5},{5,9},{9,... | collective-permute-start | bytes 98312 | tf_op jit(solution)/shard_map/ppermute | solution.py:16
  156.0 3.5 %collective-permute-done.11 = bf16[1,128,128]{1,2,0:T(8,128)(2,1)S(1)} collective-permute-done((bf16[1,128,128]{1,2,0:T(8,128)(2,1)S(1)}, bf16[1,128,128]{1,2,0:T(8,128)(2,1)S(1)}, u32[]{:S(2)}, u32[]{:S(2)}) %collective-permute-start.11) | collective-permute-done | bytes 32800 | tf_op jit(solution)/shard_map/ppermute | solution.py:16
  (80 shorter events, 16.0 us)
Async XLA Ops:
  6.5 68.6 %all-reduce.3.cloned.1.call-start = ((), (), s32[]{:S(2)}) async-start(), calls=%async_computation | async-start | bytes 524288 | tf_op jit(solution)/shard_map/psum | solution.py:65
  7.9 11.1 %copy-start.5 = (s32[4,4,5]{2,1,0:T(4,128)S(1)}, s32[4,4,5]{2,1,0:T(4,128)}, u32[]{:S(2)}) copy-start(s32[4,4,5]{2,1,0:T(4,128)} %param.9) | copy-start | bytes 964
  7.9 11.3 %copy-start.6 = (s32[4,4]{1,0:T(4,128)S(1)}, s32[4,4]{1,0:T(4,128)}, u32[]{:S(2)}) copy-start(s32[4,4]{1,0:T(4,128)} %param.10) | copy-start | bytes 196
  7.9 11.6 %copy-start.3 = (bf16[2,4,128,128]{3,2,1,0:T(8,128)(2,1)S(1)}, bf16[2,4,128,128]{3,2,1,0:T(8,128)(2,1)}, u32[]{:S(2)}) copy-start(bf16[2,4,128,128]{3,2,1,0:T(8,128)(2,1)} %param.6) | copy-start | bytes 786436
  7.9 13.2 %collective-permute-start.1 = (bf16[4,4,128,128]{2,3,1,0:T(8,128)(2,1)S(1)}, bf16[4,4,128,128]{2,3,1,0:T(8,128)(2,1)S(1)}, u32[]{:S(2)}, u32[]{:S(2)}) collective-permute-start(bf16[4,4,128,128]{2,3,1,0:T(8,128)(2,1)S(1)} %copy.8), channel_id=1, source_target_pairs={{4,0},{8,4},{12,8},{16,12},{20,16},{24,20},{28,24},{5,1},{9,5},{13... | collective-permute-start | bytes 1572872 | tf_op jit(solution)/shard_map/ppermute | solution.py:19
  10.8 13.3 %collective-permute-start = (bf16[4,4,128,128]{2,3,1,0:T(8,128)(2,1)S(1)}, bf16[4,4,128,128]{2,3,1,0:T(8,128)(2,1)S(1)}, u32[]{:S(2)}, u32[]{:S(2)}) collective-permute-start(bf16[4,4,128,128]{2,3,1,0:T(8,128)(2,1)S(1)} %copy.8), channel_id=1, source_target_pairs={{0,4},{4,8},{8,12},{12,16},{16,20},{20,24},{24,28},{1,5},{5,9},{9,... | collective-permute-start | bytes 1572872 | tf_op jit(solution)/shard_map/ppermute | solution.py:16
  24.4 75.7 %collective-permute-start.8 = (bf16[12,128,128]{1,2,0:T(8,128)(2,1)S(1)}, bf16[12,128,128]{1,2,0:T(8,128)(2,1)}, u32[]{:S(2)}, u32[]{:S(2)}) collective-permute-start(bf16[12,128,128]{1,2,0:T(8,128)(2,1)S(1)} %get-tuple-element.7), channel_id=1, source_target_pairs={{0,1},{1,2},{2,3},{4,5},{5,6},{6,7},{8,9},{9,10},{10,11},{12,13},{... | collective-permute-start | bytes 1179656 | tf_op jit(solution)/shard_map/ppermute | solution.py:27
  35.3 3.4 %copy-start.1 = (bf16[20,128,128]{1,2,0:T(8,128)(2,1)S(1)}, bf16[20,128,128]{1,2,0:T(8,128)(2,1)}, u32[]{:S(2)}) copy-start(bf16[20,128,128]{1,2,0:T(8,128)(2,1)} %gather_fusion.1) | copy-start | bytes 1966084
  35.3 3.4 %copy-start.7 = (bf16[4,4,5,128,128]{4,3,2,1,0:T(8,128)(2,1)S(1)}, bf16[4,4,5,128,128]{4,3,2,1,0:T(8,128)(2,1)}, u32[]{:S(2)}) copy-start(bf16[4,4,5,128,128]{4,3,2,1,0:T(8,128)(2,1)} %param.8) | copy-start | bytes 7864324
  36.9 2.2 %copy-start.2 = (bf16[20,128,128]{1,2,0:T(8,128)(2,1)S(1)}, bf16[20,128,128]{1,2,0:T(8,128)(2,1)}, u32[]{:S(2)}) copy-start(bf16[20,128,128]{1,2,0:T(8,128)(2,1)} %gather_fusion) | copy-start | bytes 1966084
  40.3 101.4 %all-reduce.5.cloned.1.call-start = ((), (), s32[]{:S(2)}) async-start(), calls=%async_computation.1 | async-start | bytes 524288 | tf_op jit(solution)/shard_map/psum | solution.py:65
  41.8 36.4 %copy-start = (bf16[4,3,128,128]{3,2,1,0:T(8,128)(2,1)S(1)}, bf16[4,3,128,128]{3,2,1,0:T(8,128)(2,1)}, u32[]{:S(2)}) copy-start(bf16[4,3,128,128]{3,2,1,0:T(8,128)(2,1)} %param.11) | copy-start | bytes 1179652
  76.1 17.9 %copy-start.4 = (f32[4,128,128]{1,2,0:T(8,128)S(1)}, f32[4,128,128]{1,2,0:T(8,128)}, u32[]{:S(2)}) copy-start(f32[4,128,128]{1,2,0:T(8,128)} %all-reduce.3.cloned.1.call-done) | copy-start | bytes 786436
  76.2 4.7 %collective-permute-start.3 = (bf16[1,128,128]{1,2,0:T(8,128)(2,1)S(1)}, bf16[1,128,128]{1,2,0:T(8,128)(2,1)S(1)}, u32[]{:S(2)}, u32[]{:S(2)}) collective-permute-start(bf16[1,128,128]{1,2,0:T(8,128)(2,1)S(1)} %get-tuple-element.20), channel_id=1, source_target_pairs={{4,0},{8,4},{12,8},{16,12},{20,16},{24,20},{28,24},{5,1},{9,5},{13... | collective-permute-start | bytes 98312 | tf_op jit(solution)/shard_map/ppermute | solution.py:19
  78.4 6.1 %collective-permute-start.2 = (bf16[1,128,128]{1,2,0:T(8,128)(2,1)S(1)}, bf16[1,128,128]{1,2,0:T(8,128)(2,1)S(1)}, u32[]{:S(2)}, u32[]{:S(2)}) collective-permute-start(bf16[1,128,128]{1,2,0:T(8,128)(2,1)S(1)} %get-tuple-element.19), channel_id=1, source_target_pairs={{0,4},{4,8},{8,12},{12,16},{16,20},{20,24},{24,28},{1,5},{5,9},{9,... | collective-permute-start | bytes 98312 | tf_op jit(solution)/shard_map/ppermute | solution.py:16
  85.8 4.6 %collective-permute-start.5 = (bf16[1,128,128]{1,2,0:T(8,128)(2,1)S(1)}, bf16[1,128,128]{1,2,0:T(8,128)(2,1)S(1)}, u32[]{:S(2)}, u32[]{:S(2)}) collective-permute-start(bf16[1,128,128]{1,2,0:T(8,128)(2,1)S(1)} %get-tuple-element.18), channel_id=1, source_target_pairs={{4,0},{8,4},{12,8},{16,12},{20,16},{24,20},{28,24},{5,1},{9,5},{13... | collective-permute-start | bytes 98312 | tf_op jit(solution)/shard_map/ppermute | solution.py:19
  87.9 6.1 %collective-permute-start.4 = (bf16[1,128,128]{1,2,0:T(8,128)(2,1)S(1)}, bf16[1,128,128]{1,2,0:T(8,128)(2,1)S(1)}, u32[]{:S(2)}, u32[]{:S(2)}) collective-permute-start(bf16[1,128,128]{1,2,0:T(8,128)(2,1)S(1)} %get-tuple-element.17), channel_id=1, source_target_pairs={{0,4},{4,8},{8,12},{12,16},{16,20},{20,24},{24,28},{1,5},{5,9},{9,... | collective-permute-start | bytes 98312 | tf_op jit(solution)/shard_map/ppermute | solution.py:16
  94.3 5.9 %collective-permute-start.7 = (bf16[4,128,128]{1,2,0:T(8,128)(2,1)S(1)}, bf16[4,128,128]{1,2,0:T(8,128)(2,1)S(1)}, u32[]{:S(2)}, u32[]{:S(2)}) collective-permute-start(bf16[4,128,128]{1,2,0:T(8,128)(2,1)S(1)} %fusion.25), channel_id=1, source_target_pairs={{4,0},{8,4},{12,8},{16,12},{20,16},{24,20},{28,24},{5,1},{9,5},{13... | collective-permute-start | bytes 393224 | tf_op jit(solution)/shard_map/ppermute | solution.py:19
  96.2 7.2 %collective-permute-start.6 = (bf16[4,128,128]{1,2,0:T(8,128)(2,1)S(1)}, bf16[4,128,128]{1,2,0:T(8,128)(2,1)S(1)}, u32[]{:S(2)}, u32[]{:S(2)}) collective-permute-start(bf16[4,128,128]{1,2,0:T(8,128)(2,1)S(1)} %fusion.25), channel_id=1, source_target_pairs={{0,4},{4,8},{8,12},{12,16},{16,20},{20,24},{24,28},{1,5},{5,9},{9,... | collective-permute-start | bytes 393224 | tf_op jit(solution)/shard_map/ppermute | solution.py:16
  142.7 4.6 %collective-permute-start.10 = (bf16[1,128,128]{1,2,0:T(8,128)(2,1)S(1)}, bf16[1,128,128]{1,2,0:T(8,128)(2,1)S(1)}, u32[]{:S(2)}, u32[]{:S(2)}) collective-permute-start(bf16[1,128,128]{1,2,0:T(8,128)(2,1)S(1)} %get-tuple-element.16), channel_id=1, source_target_pairs={{4,0},{8,4},{12,8},{16,12},{20,16},{24,20},{28,24},{5,1},{9,5},{13... | collective-permute-start | bytes 98312 | tf_op jit(solution)/shard_map/ppermute | solution.py:19
  144.8 6.1 %collective-permute-start.9 = (bf16[1,128,128]{1,2,0:T(8,128)(2,1)S(1)}, bf16[1,128,128]{1,2,0:T(8,128)(2,1)S(1)}, u32[]{:S(2)}, u32[]{:S(2)}) collective-permute-start(bf16[1,128,128]{1,2,0:T(8,128)(2,1)S(1)} %get-tuple-element.15), channel_id=1, source_target_pairs={{0,4},{4,8},{8,12},{12,16},{16,20},{20,24},{24,28},{1,5},{5,9},{9,... | collective-permute-start | bytes 98312 | tf_op jit(solution)/shard_map/ppermute | solution.py:16
  151.2 4.6 %collective-permute-start.12 = (bf16[1,128,128]{1,2,0:T(8,128)(2,1)S(1)}, bf16[1,128,128]{1,2,0:T(8,128)(2,1)S(1)}, u32[]{:S(2)}, u32[]{:S(2)}) collective-permute-start(bf16[1,128,128]{1,2,0:T(8,128)(2,1)S(1)} %get-tuple-element.14), channel_id=1, source_target_pairs={{4,0},{8,4},{12,8},{16,12},{20,16},{24,20},{28,24},{5,1},{9,5},{13... | collective-permute-start | bytes 98312 | tf_op jit(solution)/shard_map/ppermute | solution.py:19
  153.4 6.1 %collective-permute-start.11 = (bf16[1,128,128]{1,2,0:T(8,128)(2,1)S(1)}, bf16[1,128,128]{1,2,0:T(8,128)(2,1)S(1)}, u32[]{:S(2)}, u32[]{:S(2)}) collective-permute-start(bf16[1,128,128]{1,2,0:T(8,128)(2,1)S(1)} %get-tuple-element.13), channel_id=1, source_target_pairs={{0,4},{4,8},{8,12},{12,16},{16,20},{20,24},{24,28},{1,5},{5,9},{9,... | collective-permute-start | bytes 98312 | tf_op jit(solution)/shard_map/ppermute | solution.py:16
Sparse Core Ops, SparseCore 0:
  40.4 34.7 all-reduce.2
  106.5 35.1 all-reduce.4
where the time goes:
time: 168 us; the launch traced here: 167 us
  waiting for transfers between devices  87.9 us (52%)
  starting transfers between devices  30.9 us (18%)
  local copies, waits for them, and re-layouts  16.2 us (10%)
  matrix products  15.1 us (9%)
  between operations  13.9 us (8%)
  other arithmetic  3.21 us (2%)
    psum x2, waiting for transfers between devices, settle(): field = lax.psum(partial_value, 'hist')  66.3 us
    ppermute x6, waiting for transfers between devices, extended(): lax.ppermute(lax.slice_in_dim(block, block.shape[dim] - width, None, axis...  20.3 us
    ppermute x6, starting transfers between devices, extended(): lax.ppermute(lax.slice_in_dim(block, block.shape[dim] - width, None, axis...  14 us
    ppermute x6, starting transfers between devices, extended(): lax.ppermute(lax.slice_in_dim(block, 0, width, axis=dim), axis, backward)  12.6 us
    dot_general x8, matrix products, shell_field(): jnp.einsum('nsij,nsjp->nip', tiles, taken, preferred_element_type=jnp.flo...  11.6 us
    gather x8, local copies, waits for them, and re-layouts, shell_field(): taken = shell_rim[index]  7.91 us
    ppermute x1, starting transfers between devices, shifted_2(): return lax.ppermute(value, axis, pairs)  4.24 us
    squeeze x2, local copies, waits for them, and re-layouts, shards(): near_tiles[:, 1]  4.16 us
  transfers between devices with their start and end apart: 15, of which 9 were waited for; matrix products, arithmetic and copies ran while one was open for 17% of the time, Pallas kernels for 0%

commit v1 on v0

v1 whole, which is shorter than its diff:
```python
import functools

import jax
import jax.numpy as jnp
from jax import lax
from jax.experimental import pallas as pl
from jax.experimental.pallas import tpu as pltpu
from jax.sharding import PartitionSpec as P

WIN = 4
MESH = pl.DeviceIdType.MESH
F32 = jnp.float32
BF16 = jnp.bfloat16
NT = (((1,), (1,)), ((), ()))


def kernel(
    panels_n, hist_n,
    exc_ref, past_ref, tiles_ref, src_hbm, count_hbm, near_ref, src_ref, count_ref,
    out_ref,
    c0, c1, c2, c3, cprev, tv, t0, ne, exv, acc, drive, rs_out, rs_in, rs_out2, rs_in2,
    xe, xe2, cu, srcv, countv, srcs, counts,
    past_s, past_r, zown_s, zown_r, cp_s, cp_r, t0_s, t0_r, ix_s, ix_r, ne_s, ne_r,
    rs_s, rs_r, rs2_s, rs2_r, xe_s, xe_r, xe2_s, xe2_r, cu_s, cu_r,
    lpast, ltile, lnear, lexc, lt0, lix,
):
    cs = (c0, c1, c2, c3)
    shells, blocks, slots = tiles_ref.shape[:3]
    size = tiles_ref.shape[3]
    share = out_ref.shape[2]
    me = lax.axis_index("panel")
    zed = lax.axis_index("hist")
    has_l, has_r = me > 0, me < panels_n - 1
    has_d, has_u = zed > 0, zed < hist_n - 1
    none = blocks + 2 * WIN

    def when(condition, action):
        pl.when(condition)(action)

    local_past = [
        pltpu.make_async_copy(past_ref.at[k], cs[k].at[pl.ds(WIN, blocks)], lpast.at[k])
        for k in range(shells)
    ]
    local_tile = [
        pltpu.make_async_copy(tiles_ref.at[k], tv.at[k], ltile.at[k]) for k in range(shells)
    ]
    local_near = pltpu.make_async_copy(near_ref, ne.at[pl.ds(1, blocks)], lnear)
    local_exc = pltpu.make_async_copy(exc_ref, exv, lexc)
    local_t0 = pltpu.make_async_copy(tiles_ref.at[0], t0, lt0)
    local_ix = [
        pltpu.make_async_copy(src_hbm.at[0], srcv, lix.at[0]),
        pltpu.make_async_copy(count_hbm, countv, lix.at[1]),
    ]

    def pair(send, recv, out_right, in_left, out_left, in_right):
        right = pltpu.make_async_remote_copy(
            src_ref=out_right, dst_ref=in_left, send_sem=send.at[0], recv_sem=recv.at[0],
            device_id={"panel": jnp.minimum(me + 1, panels_n - 1)}, device_id_type=MESH,
        )
        left = pltpu.make_async_remote_copy(
            src_ref=out_left, dst_ref=in_right, send_sem=send.at[1], recv_sem=recv.at[1],
            device_id={"panel": jnp.maximum(me - 1, 0)}, device_id_type=MESH,
        )
        return right, left

    def pair_start(p):
        when(has_r, p[0].start)
        when(has_l, p[1].start)

    def pair_recv(p):
        when(has_l, p[0].wait_recv)
        when(has_r, p[1].wait_recv)

    def pair_send(p):
        when(has_r, p[0].wait_send)
        when(has_l, p[1].wait_send)

    low, high = pl.ds(0, WIN), pl.ds(WIN + blocks, WIN)
    first, last = pl.ds(WIN, WIN), pl.ds(blocks, WIN)
    past_pairs = [
        pair(
            past_s.at[k], past_r.at[k],
            past_ref.at[k, pl.ds(blocks - WIN, WIN)], cs[k].at[low],
            past_ref.at[k, pl.ds(0, WIN)], cs[k].at[high],
        )
        for k in range(shells)
    ]
    cp_pair = pair(cp_s, cp_r, cprev.at[last], cprev.at[low], cprev.at[first], cprev.at[high])
    near_pair = pair(
        ne_s, ne_r, near_ref.at[blocks - 1], ne.at[0], near_ref.at[0], ne.at[blocks + 1]
    )
    xe_out = (pl.ds(blocks, 2), pl.ds(0, 2), pl.ds(2, 2), pl.ds(blocks + 2, 2))
    xe_pair = pair(xe_s, xe_r, *[xe.at[w] for w in xe_out])
    xe2_pair = pair(xe2_s, xe2_r, *[xe2.at[w] for w in xe_out])
    cu_pair = pair(cu_s, cu_r, cu.at[last], cu.at[low], cu.at[first], cu.at[high])

    above = {"hist": jnp.minimum(zed + 1, hist_n - 1)}
    zown = pltpu.make_async_remote_copy(
        src_ref=past_ref.at[shells - 1], dst_ref=cprev.at[pl.ds(WIN, blocks)],
        send_sem=zown_s, recv_sem=zown_r, device_id=above, device_id_type=MESH,
    )

    def t0_copy(chunk, source):
        return pltpu.make_async_remote_copy(
            src_ref=source, dst_ref=t0.at[chunk], send_sem=t0_s.at[chunk],
            recv_sem=t0_r.at[chunk], device_id=above, device_id_type=MESH,
        )

    def t0_forward(chunk):
        def go():
            copy = t0_copy(chunk, t0.at[chunk])
            copy.wait_recv()
            when(has_u, copy.start)
        return go

    def t0_point(where):
        for chunk in range(blocks):
            for at in range(1, 4):
                when_at = {1: 1 + chunk, 2: 3 + chunk - (chunk > 1), 3: 5}[at]
                when_at = min(when_at, 5)
                if when_at == where:
                    when((zed == at) if at < 3 else (zed >= at), t0_forward(chunk))

    ix_copies = []
    for other in range(1, hist_n):
        ix_copies.append([
            pltpu.make_async_remote_copy(
                src_ref=source, dst_ref=target, send_sem=ix_s.at[other - 1, j],
                recv_sem=ix_r.at[j], device_id={"hist": other}, device_id_type=MESH,
            )
            for j, (source, target) in enumerate(((src_hbm.at[0], srcv), (count_hbm, countv)))
        ])

    def reduce_copies(send, recv, out, into):
        copies = []
        for step in range(1, hist_n):
            other = lax.rem(zed + step, hist_n)
            copies.append(pltpu.make_async_remote_copy(
                src_ref=out.at[other], dst_ref=into.at[step - 1],
                send_sem=send.at[step - 1], recv_sem=recv.at[step - 1],
                device_id={"hist": other}, device_id_type=MESH,
            ))
        return copies

    rs_copies = reduce_copies(rs_s, rs_r, rs_out, rs_in)
    rs2_copies = reduce_copies(rs2_s, rs2_r, rs_out2, rs_in2)

    for copy in local_past + [local_near, local_exc] + local_tile:
        copy.start()

    def at_zero():
        local_t0.start()
        for copy in local_ix:
            copy.start()
    when(zed == 0, at_zero)

    barrier = pltpu.get_barrier_semaphore()

    def greet(device):
        return lambda: pl.semaphore_signal(
            barrier, inc=1, device_id=device, device_id_type=MESH
        )
    when(has_r, greet({"panel": jnp.minimum(me + 1, panels_n - 1)}))
    when(has_l, greet({"panel": jnp.maximum(me - 1, 0)}))
    for step in range(1, hist_n):
        greet({"hist": lax.rem(zed + step, hist_n)})()
    for c in cs + (cprev,):
        c[none] = jnp.zeros((size, size), BF16)
    cu[none] = jnp.zeros((share, size), BF16)
    pl.semaphore_wait(
        barrier, hist_n - 1 + has_r.astype(jnp.int32) + has_l.astype(jnp.int32)
    )

    for p in past_pairs:
        pair_start(p)

    def spread():
        for copies in ix_copies:
            for copy in copies:
                copy.start()
        for chunk in range(blocks):
            t0_copy(chunk, tiles_ref.at[0, chunk]).start()
    when(zed == 0, spread)
    when(has_u, zown.start)

    local_exc.wait()
    for t in range(2):
        for n in range(blocks):
            drive[t, n] = exv[t, n].astype(F32).T
    local_near.wait()
    eye = lax.broadcasted_iota(jnp.int32, (size, size), 0) == lax.broadcasted_iota(
        jnp.int32, (size, size), 1
    )

    def diagonal(tile):
        return jnp.sum(jnp.where(eye, tile.astype(F32), 0.0), axis=0, keepdims=True)

    diag = {e: diagonal(ne[e, 1]) for e in range(1, blocks + 1)}

    def place(source, count, n, s):
        block = me * blocks + n + source
        live = (s < count) & (block >= 0) & (block < panels_n * blocks)
        return jnp.where(live, n + source + WIN, none)

    def tile_row(ref, n):
        return jnp.concatenate([ref[n, s] for s in range(slots)], axis=1)

    for k in range(shells):
        local_past[k].wait()
        local_tile[k].wait()
        pair_recv(past_pairs[k])
        if k == 2:
            pair_start(near_pair)
        for n in range(blocks):
            at = [place(src_ref[k, n, s], count_ref[k, n], n, s) for s in range(slots)]
            left = tile_row(tv.at[k], n)
            right = jnp.concatenate([cs[k][i] for i in at], axis=0)
            if k > 0:
                older = jnp.concatenate([cs[k - 1][i] for i in at], axis=0)
                right = jnp.concatenate([right, older], axis=1)
            part = jnp.dot(left, right, preferred_element_type=F32)
            if k == 0:
                acc[n, :, pl.ds(0, size)] = part
            elif k == 1:
                acc[n, :, pl.ds(0, size)] += part[:, :size]
                acc[n, :, pl.ds(size, size)] = part[:, size:]
            else:
                acc[n] += part
        t0_point(k)

    mine = pl.ds(pl.multiple_of(zed * share, share), share)

    for n in range(blocks):
        field = acc[n, :, pl.ds(0, size)].T
        drive[0, n] -= field
        rs_out[:, n] = field.reshape(hist_n, share, size).astype(BF16)
    for copy in rs_copies:
        copy.start()

    def pass_on():
        zown.wait_recv()
        pair_start(cp_pair)
    when(has_d, pass_on)
    for copy in rs_copies:
        copy.wait_recv()

    def driven(t, n, into):
        g = drive[t, n, mine]
        for step in range(hist_n - 1):
            g = g - into[step, n].astype(F32)
        return g

    def begin(g, states, copy_pair):
        x = [g[n] / diag[n + 1] for n in range(blocks)]
        for n in range(blocks):
            states[n + 2] = x[n].astype(BF16)
        pair_start(copy_pair)
        return x

    g = [driven(0, n, rs_in) for n in range(blocks)]
    x = begin(g, xe, xe_pair)
    t0_point(4)

    def older_shell():
        pair_recv(cp_pair)
        for n in range(blocks):
            at = [place(src_ref[0, n, s], count_ref[0, n], n, s) for s in range(slots)]
            right = jnp.concatenate([cprev[i] for i in at], axis=0)
            acc[n, :, pl.ds(size, size)] += jnp.dot(
                tile_row(tv.at[0], n), right, preferred_element_type=F32
            )
    when(has_d, older_shell)
    for n in range(blocks):
        field = acc[n, :, pl.ds(size, size)].T
        drive[1, n] -= field
        rs_out2[:, n] = field.reshape(hist_n, share, size).astype(BF16)
    for copy in rs2_copies:
        copy.start()
    pair_recv(near_pair)
    for e in (0, blocks + 1):
        diag[e] = diagonal(ne[e, 1])

    def applied(states, e):
        tiles = jnp.concatenate([ne[e, j] for j in range(3)], axis=1)
        return lax.dot_general(
            jnp.concatenate(states, axis=1), tiles, NT, preferred_element_type=F32
        )

    def sweeps(g, x, states, copy_pair):
        pair_recv(copy_pair)
        empty = jnp.zeros((share, size), BF16)
        held = [states[j] for j in range(blocks + 4)]
        for j in range(2):
            held[j] = jnp.where(has_l, held[j], empty)
            held[blocks + 2 + j] = jnp.where(has_r, held[blocks + 2 + j], empty)
        new = []
        for e in range(blocks + 2):
            by = applied(held[e : e + 3], e)
            if 0 < e <= blocks:
                x[e - 1] = x[e - 1] + (g[e - 1] - by) / diag[e]
                new.append(x[e - 1].astype(BF16))
            else:
                start = held[e + 1].astype(F32)
                value = (start + (start - by / diag[e])).astype(BF16)
                new.append(jnp.where(has_l if e == 0 else has_r, value, empty))
        return [
            (x[n] + (g[n] - applied(new[n : n + 3], n + 1)) / diag[n + 1]).astype(BF16)
            for n in range(blocks)
        ]

    now = sweeps(g, x, xe, xe_pair)
    for n in range(blocks):
        cu[WIN + n] = now[n]
    pair_start(cu_pair)
    for n in range(blocks):
        out_ref[0, n] = now[n]
    t0_point(5)

    def here():
        local_t0.wait()
        for copy in local_ix:
            copy.wait()

    def there():
        for copy in ix_copies[0]:
            copy.wait_recv()
    when(zed == 0, here)
    when(zed > 0, there)
    to_scalar = [
        pltpu.make_async_copy(srcv, srcs, lix.at[2]),
        pltpu.make_async_copy(countv, counts, lix.at[3]),
    ]
    for copy in to_scalar:
        copy.start()
    for copy in rs2_copies:
        copy.wait_recv()
    g = [driven(1, n, rs_in2) for n in range(blocks)]
    for copy in to_scalar:
        copy.wait()
    pair_recv(cu_pair)
    for n in range(blocks):
        at = [place(srcs[n, s], counts[0, n], n, s) for s in range(slots)]
        left = jnp.concatenate([cu[i] for i in at], axis=1)
        g[n] = g[n] - lax.dot_general(
            left, tile_row(t0, n), NT, preferred_element_type=F32
        )
    x = begin(g, xe2, xe2_pair)
    now = sweeps(g, x, xe2, xe2_pair)
    for n in range(blocks):
        out_ref[1, n] = now[n]

    for p in past_pairs + [near_pair, xe_pair, xe2_pair, cu_pair]:
        pair_send(p)
    when(has_d, lambda: pair_send(cp_pair))
    for copy in rs_copies + rs2_copies:
        copy.wait_send()
    when(has_u, zown.wait_send)

    def t0_sent():
        for chunk in range(blocks):
            t0_copy(chunk, t0.at[chunk]).wait_send()
    when(has_u, t0_sent)

    def ix_sent():
        for copies in ix_copies:
            for copy in copies:
                copy.wait_send()
    when(zed == 0, ix_sent)


def shards(panels_n, hist_n, excitation, past, hist_tiles, hist_src, hist_count, near_tiles):
    shells, blocks, slots, size = hist_tiles.shape[:4]
    ports = past.shape[3]
    share = ports // hist_n
    any_space = pl.BlockSpec(memory_space=pl.ANY)
    scalar = pl.BlockSpec(memory_space=pltpu.SMEM)
    span = blocks + 2 * WIN + 1
    dma = pltpu.SemaphoreType.DMA
    vmem = pltpu.VMEM
    out = pl.pallas_call(
        functools.partial(kernel, panels_n, hist_n),
        out_shape=jax.ShapeDtypeStruct((2, blocks, share, size), BF16),
        in_specs=[any_space] * 6 + [scalar] * 2,
        out_specs=pl.BlockSpec(memory_space=pltpu.VMEM),
        scratch_shapes=[vmem((span, size, ports), BF16)] * 5
        + [
            vmem((shells, blocks, slots, size, size), BF16),
            vmem((blocks, slots, size, size), BF16),
            vmem((blocks + 2, 3, size, size), BF16),
            vmem((2, blocks, size, ports), BF16),
            vmem((blocks, size, 2 * ports), F32),
            vmem((2, blocks, ports, size), F32),
        ]
        + [
            vmem((hist_n, blocks, share, size), BF16),
            vmem((hist_n - 1, blocks, share, size), BF16),
        ] * 2
        + [
            vmem((blocks + 4, share, size), BF16),
            vmem((blocks + 4, share, size), BF16),
            vmem((span, share, size), BF16),
            vmem((blocks, slots), jnp.int32),
            vmem((shells, blocks), jnp.int32),
            pltpu.SMEM((blocks, slots), jnp.int32),
            pltpu.SMEM((shells, blocks), jnp.int32),
            dma((shells, 2)), dma((shells, 2)),
            dma, dma,
            dma((2,)), dma((2,)),
            dma((blocks,)), dma((blocks,)),
            dma((hist_n - 1, 2)), dma((2,)),
            dma((2,)), dma((2,)),
            dma((hist_n - 1,)), dma((hist_n - 1,)),
            dma((hist_n - 1,)), dma((hist_n - 1,)),
            dma((2,)), dma((2,)), dma((2,)), dma((2,)), dma((2,)), dma((2,)),
            dma((shells,)), dma((shells,)), dma, dma, dma, dma((4,)),
        ],
        compiler_params=pltpu.CompilerParams(
            collective_id=0, has_side_effects=True, vmem_limit_bytes=40 * 1024 * 1024
        ),
    )(excitation, past, hist_tiles, hist_src, hist_count, near_tiles, hist_src, hist_count)
    return jnp.swapaxes(out, 2, 3)


def solution(mesh):
    return jax.shard_map(
        functools.partial(shards, mesh.shape["panel"], mesh.shape["hist"]),
        mesh=mesh,
        in_specs=(
            P(None, "panel", None, None),
            P("hist", "panel", None, None),
            P("hist", "panel", None, None, None),
            P("hist", "panel", None),
            P("hist", "panel"),
            P("panel", None, None, None),
        ),
        out_specs=P(None, "panel", None, "hist"),
        check_vma=False,
    )
```

time: 168 us -> 52.5 us (0.31)
  the two profiles are of different devices: /device:TPU:4 before, /device:TPU:25 now
where the time goes in v1:
time: 52.5 us; the launch traced here: 52.1 us
  Pallas kernels  45.4 us (86%)
  local copies, waits for them, and re-layouts  6.73 us (13%)
    pallas_call x1, Pallas kernels, shards(): pl.pallas_call(functools.partial(kernel, panels_n, hist_n), out_shape=jax...  45.4 us
    unnamed x13, local copies, waits for them, and re-layouts  6.73 us

profile of v1, /device:TPU:25, one launch (start us, length us, event | category | flops | bytes accessed | tf_op | source)
XLA Modules:
  0.0 52.1 jit_solution(8385487153866441445)
XLA Ops:
  0.0 0.0 copy-start
  0.0 1.7 %copy-done = bf16[4,4,5,128,128]{4,3,2,1,0:T(8,128)(2,1)S(1)} copy-done((bf16[4,4,5,128,128]{4,3,2,1,0:T(8,128)(2,1)S(1)}, bf16[4,4,5,128,128]{4,3,2,1,0:T(8,128)(2,1)}, u32[]{:S(2)}) %copy-start) | copy-done | bytes 2621464
  1.7 0.0 copy-start.1
  1.7 1.0 %copy-done.1 = bf16[4,4,128,128]{3,2,1,0:T(8,128)(2,1)S(1)} copy-done((bf16[4,4,128,128]{3,2,1,0:T(8,128)(2,1)S(1)}, bf16[4,4,128,128]{3,2,1,0:T(8,128)(2,1)}, u32[]{:S(2)}) %copy-start.1) | copy-done | bytes 524312
  2.8 0.0 copy-start.2
  2.8 1.0 %copy-done.2 = bf16[4,3,128,128]{3,2,1,0:T(8,128)(2,1)S(1)} copy-done((bf16[4,3,128,128]{3,2,1,0:T(8,128)(2,1)S(1)}, bf16[4,3,128,128]{3,2,1,0:T(8,128)(2,1)}, u32[]{:S(2)}) %copy-start.2) | copy-done | bytes 393240
  3.8 0.0 copy-start.3
  3.8 0.9 %copy-done.3 = bf16[2,4,128,128]{3,2,1,0:T(8,128)(2,1)S(1)} copy-done((bf16[2,4,128,128]{3,2,1,0:T(8,128)(2,1)S(1)}, bf16[2,4,128,128]{3,2,1,0:T(8,128)(2,1)}, u32[]{:S(2)}) %copy-start.3) | copy-done | bytes 262168
  4.7 0.0 copy-start.4
  4.7 0.7 %copy-done.4 = s32[4,4,5]{2,1,0:T(4,128)S(1)} copy-done((s32[4,4,5]{2,1,0:T(4,128)S(1)}, s32[4,4,5]{2,1,0:T(4,128)}, u32[]{:S(2)}) %copy-start.4) | copy-done | bytes 344
  5.4 0.0 copy-start.5
  5.4 0.7 %copy-done.5 = s32[4,4]{1,0:T(4,128)S(1)} copy-done((s32[4,4]{1,0:T(4,128)S(1)}, s32[4,4]{1,0:T(4,128)}, u32[]{:S(2)}) %copy-start.5) | copy-done | bytes 88
  6.1 45.4 %shard_map.64 = bf16[2,4,32,128]{3,2,1,0:T(8,128)(2,1)S(1)} custom-call(bf16[2,4,128,128]{3,2,1,0:T(8,128)(2,1)S(1)} %copy-done.3, bf16[4,4,128,128]{3,2,1,0:T(8,128)(2,1)S(1)} %copy-done.1, bf16[4,4,5,128,128]{4,3,2,1,0:T(8,128)(2,1)S(1)} %copy-done, s32[4,4,5]{2,1,0:T(4,128)S(1)} %copy-done.4, s32[4,4]{1,0:T(4,128)S(1)} %copy-done.5, ...), custom_call_target="tpu_custom_call" | custom-call | tf_op jit(solution)/shard_map/pallas_call | solution.py:380
  51.5 0.6 %copy.8 = bf16[2,4,128,32]{2,3,1,0:T(8,128)(2,1)} copy(bf16[2,4,128,32]{2,3,1,0:T(8,128)(2,1)S(1)} %bitcast.1) | data formatting | bytes 131072
Async XLA Ops:
  0.0 1.7 %copy-start = (bf16[4,4,5,128,128]{4,3,2,1,0:T(8,128)(2,1)S(1)}, bf16[4,4,5,128,128]{4,3,2,1,0:T(8,128)(2,1)}, u32[]{:S(2)}) copy-start(bf16[4,4,5,128,128]{4,3,2,1,0:T(8,128)(2,1)} %tiles_ref.1) | copy-start | bytes 7864324
  1.7 1.0 %copy-start.1 = (bf16[4,4,128,128]{3,2,1,0:T(8,128)(2,1)S(1)}, bf16[4,4,128,128]{3,2,1,0:T(8,128)(2,1)}, u32[]{:S(2)}) copy-start(bf16[4,4,128,128]{3,2,1,0:T(8,128)(2,1)} %past_ref.1) | copy-start | bytes 1572868
  2.8 1.0 %copy-start.2 = (bf16[4,3,128,128]{3,2,1,0:T(8,128)(2,1)S(1)}, bf16[4,3,128,128]{3,2,1,0:T(8,128)(2,1)}, u32[]{:S(2)}) copy-start(bf16[4,3,128,128]{3,2,1,0:T(8,128)(2,1)} %near_ref.1) | copy-start | bytes 1179652
  3.8 0.9 %copy-start.3 = (bf16[2,4,128,128]{3,2,1,0:T(8,128)(2,1)S(1)}, bf16[2,4,128,128]{3,2,1,0:T(8,128)(2,1)}, u32[]{:S(2)}) copy-start(bf16[2,4,128,128]{3,2,1,0:T(8,128)(2,1)} %exc_ref.1) | copy-start | bytes 786436
  4.7 0.7 %copy-start.4 = (s32[4,4,5]{2,1,0:T(4,128)S(1)}, s32[4,4,5]{2,1,0:T(4,128)}, u32[]{:S(2)}) copy-start(s32[4,4,5]{2,1,0:T(4,128)} %src_ref.1) | copy-start | bytes 964
  5.4 0.7 %copy-start.5 = (s32[4,4]{1,0:T(4,128)S(1)}, s32[4,4]{1,0:T(4,128)}, u32[]{:S(2)}) copy-start(s32[4,4]{1,0:T(4,128)} %count_ref.1) | copy-start | bytes 196

commit v2 on v1

--- a/solution.py
+++ b/solution.py
@@ -110,16 +110,17 @@
         def go():
             copy = t0_copy(chunk, t0.at[chunk])
             copy.wait_recv()
-            when(has_u, copy.start)
+            copy.start()
         return go
 
     def t0_point(where):
         for chunk in range(blocks):
-            for at in range(1, 4):
-                when_at = {1: 1 + chunk, 2: 3 + chunk - (chunk > 1), 3: 5}[at]
-                when_at = min(when_at, 5)
-                if when_at == where:
-                    when((zed == at) if at < 3 else (zed >= at), t0_forward(chunk))
+            if where == (-1 if chunk < blocks - 1 else 0):
+                when((zed == 1) & has_u, t0_forward(chunk))
+            if where == (-1, 0, 3, 4)[min(chunk, 3)]:
+                when((zed == 2) & has_u, t0_forward(chunk))
+            if where == 6:
+                when((zed > 2) & has_u, t0_forward(chunk))
 
     ix_copies = []
     for other in range(1, hist_n):
@@ -205,6 +206,7 @@
     def tile_row(ref, n):
         return jnp.concatenate([ref[n, s] for s in range(slots)], axis=1)
 
+    t0_point(-1)
     for k in range(shells):
         local_past[k].wait()
         local_tile[k].wait()
@@ -241,6 +243,7 @@
         zown.wait_recv()
         pair_start(cp_pair)
     when(has_d, pass_on)
+    t0_point(4)
     for copy in rs_copies:
         copy.wait_recv()
 
@@ -259,7 +262,7 @@
 
     g = [driven(0, n, rs_in) for n in range(blocks)]
     x = begin(g, xe, xe_pair)
-    t0_point(4)
+    t0_point(5)
 
     def older_shell():
         pair_recv(cp_pair)
@@ -276,6 +279,7 @@
         rs_out2[:, n] = field.reshape(hist_n, share, size).astype(BF16)
     for copy in rs2_copies:
         copy.start()
+    t0_point(6)
     pair_recv(near_pair)
     for e in (0, blocks + 1):
         diag[e] = diagonal(ne[e, 1])
@@ -314,7 +318,6 @@
     pair_start(cu_pair)
     for n in range(blocks):
         out_ref[0, n] = now[n]
-    t0_point(5)
 
     def here():
         local_t0.wait()
@@ -324,6 +327,11 @@
     def there():
         for copy in ix_copies[0]:
             copy.wait_recv()
+
+        def parts():
+            for chunk in range(blocks):
+                t0_copy(chunk, t0.at[chunk]).wait_recv()
+        when(zed == hist_n - 1, parts)
     when(zed == 0, here)
     when(zed > 0, there)
     to_scalar = [
@@ -372,7 +380,7 @@
     shells, blocks, slots, size = hist_tiles.shape[:4]
     ports = past.shape[3]
     share = ports // hist_n
-    any_space = pl.BlockSpec(memory_space=pl.ANY)
+    any_space = pl.BlockSpec(memory_space=pltpu.HBM)
     scalar = pl.BlockSpec(memory_space=pltpu.SMEM)
     span = blocks + 2 * WIN + 1
     dma = pltpu.SemaphoreType.DMA
@@ -415,7 +423,7 @@
             dma((shells,)), dma((shells,)), dma, dma, dma, dma((4,)),
         ],
         compiler_params=pltpu.CompilerParams(
-            collective_id=0, has_side_effects=True, vmem_limit_bytes=40 * 1024 * 1024
+            collective_id=0, has_side_effects=True, vmem_limit_bytes=64 * 1024 * 1024
         ),
     )(excitation, past, hist_tiles, hist_src, hist_count, near_tiles, hist_src, hist_count)
     return jnp.swapaxes(out, 2, 3)

time: 52.5 us -> 44.6 us (0.85)
  the two profiles are of different devices: /device:TPU:25 before, /device:TPU:27 now
where the time goes in v2:
time: 44.6 us; the launch traced here: 44.4 us
  Pallas kernels  42.9 us (96%)
  local copies, waits for them, and re-layouts  1.47 us (3%)
    pallas_call x1, Pallas kernels, shards(): pl.pallas_call(functools.partial(kernel, panels_n, hist_n), out_shape=jax...  42.9 us
    unnamed x1, local copies, waits for them, and re-layouts  1.47 us

profile of v2, /device:TPU:27, one launch (start us, length us, event | category | flops | bytes accessed | tf_op | source)
XLA Modules:
  0.0 44.4 jit_solution(17190035035176618599)
XLA Ops:
  0.0 42.9 %shard_map.64 = bf16[2,4,32,128]{3,2,1,0:T(8,128)(2,1)} custom-call(bf16[2,4,128,128]{3,2,1,0:T(8,128)(2,1)} %exc_ref.1, bf16[4,4,128,128]{3,2,1,0:T(8,128)(2,1)} %past_ref.1, bf16[4,4,5,128,128]{4,3,2,1,0:T(8,128)(2,1)} %tiles_ref.1, s32[4,4,5]{2,1,0:T(4,128)} %src_ref.1, s32[4,4]{1,0:T(4,128)} %count_ref.1, bf16[4,3,128,128]{3,2,1,0:T(8,128)(2,1)} %near_ref.1, ...), custom_call_target="tpu_custom_call" | custom-call | tf_op jit(solution)/shard_map/pallas_call | solution.py:388
  42.9 1.5 %copy.8 = bf16[2,4,128,32]{2,3,1,0:T(8,128)(2,1)} copy(bf16[2,4,128,32]{2,3,1,0:T(8,128)(2,1)} %bitcast.1) | data formatting | bytes 131072

commit v3 on v2

--- a/solution.py
+++ b/solution.py
@@ -115,9 +115,9 @@
 
     def t0_point(where):
         for chunk in range(blocks):
-            if where == (-1 if chunk < blocks - 1 else 0):
+            if where == 1 + chunk:
                 when((zed == 1) & has_u, t0_forward(chunk))
-            if where == (-1, 0, 3, 4)[min(chunk, 3)]:
+            if where == 3 + chunk:
                 when((zed == 2) & has_u, t0_forward(chunk))
             if where == 6:
                 when((zed > 2) & has_u, t0_forward(chunk))
@@ -206,7 +206,6 @@
     def tile_row(ref, n):
         return jnp.concatenate([ref[n, s] for s in range(slots)], axis=1)
 
-    t0_point(-1)
     for k in range(shells):
         local_past[k].wait()
         local_tile[k].wait()

time: 44.6 us -> 43.3 us (0.971)
  the two profiles are of different devices: /device:TPU:27 before, /device:TPU:25 now
where the time goes in v3:
time: 43.3 us; the launch traced here: 43 us
  Pallas kernels  41.6 us (96%)
  local copies, waits for them, and re-layouts  1.47 us (3%)
    pallas_call x1, Pallas kernels, shards(): pl.pallas_call(functools.partial(kernel, panels_n, hist_n), out_shape=jax...  41.6 us
    unnamed x1, local copies, waits for them, and re-layouts  1.47 us

profile of v3, /device:TPU:25, one launch (start us, length us, event | category | flops | bytes accessed | tf_op | source)
XLA Modules:
  0.0 43.0 jit_solution(8715794878422977569)
XLA Ops:
  0.0 41.6 %shard_map.64 = bf16[2,4,32,128]{3,2,1,0:T(8,128)(2,1)} custom-call(bf16[2,4,128,128]{3,2,1,0:T(8,128)(2,1)} %exc_ref.1, bf16[4,4,128,128]{3,2,1,0:T(8,128)(2,1)} %past_ref.1, bf16[4,4,5,128,128]{4,3,2,1,0:T(8,128)(2,1)} %tiles_ref.1, s32[4,4,5]{2,1,0:T(4,128)} %src_ref.1, s32[4,4]{1,0:T(4,128)} %count_ref.1, bf16[4,3,128,128]{3,2,1,0:T(8,128)(2,1)} %near_ref.1, ...), custom_call_target="tpu_custom_call" | custom-call | tf_op jit(solution)/shard_map/pallas_call | solution.py:387
  41.6 1.5 %copy.8 = bf16[2,4,128,32]{2,3,1,0:T(8,128)(2,1)} copy(bf16[2,4,128,32]{2,3,1,0:T(8,128)(2,1)} %bitcast.1) | data formatting | bytes 131072
